TPU v7x, 32 devices: a whole 2x2x4 slice. The times are simulated.
32 devices in a mesh: parts: 2 (over y), bank: 4 (over z), tm: 2 (over x), rate: 2 (over core).
Axes of the slice: x: 2, y: 2, z: 4, core: 2. Of those that a mesh axis runs over, the one named last changes fastest.
Arguments:
- strain: float32 [2, 16384], P('rate', ('parts', 'bank', 'tm')), parts along dimension 1, may hold values from -6 to 6
- gate_mask: int32 [16384], P(('parts', 'bank', 'tm')), parts along dimension 0, may hold values 0 or 1
- psd_reset: int32 [16], P(('parts', 'bank', 'tm')), parts along dimension 0, may hold values from 0 to 1
- psd_ref: float32 [2, 512], P('rate'), may hold values from 0.1 to 10
- psd_rate: float32 [2, 512], P('rate'), may hold values from 0.025 to 0.5
- filters: bfloat16 [4, 2, 32, 2048], P('bank', 'rate'), may hold values from -0.125 to 0.125
- basis_count: int32 [4], P('bank'), may hold values from 16 to 32, as said below
- mixing: bfloat16 [4, 2, 4, 2, 32], P('bank', 'rate'), may hold values from -0.75 to 0.75
- autocorrelation: float32 [4, 2, 257], replicated, may hold values from -1.2 to 1.2
Outputs:
- snr_sq: float32 [4, 4, 16384], P(None, 'rate', ('parts', 'bank', 'tm')), parts along dimension 2
- chisq: float32 [4, 4, 16384], P(None, 'rate', ('parts', 'bank', 'tm')), parts along dimension 2
There are 2 independent parts, one for each index of `parts`. A program takes and returns all parts, laid end to end along the dimension named above; an argument that names none is the same for every part. Nothing has to cross between parts.
Inputs may be any that keep to these rules, and one draw needn't show every extreme that they name: `basis_count`: some bank uses all 32 basis filters and another only half of them.
All inputs are finite; a program needn't handle non-finite values. No bound on the sum of `gate_mask` on one device may be relied on, other than what follows from the above.
Results may differ from a plain program's by a relative error of at most 0.0044.
Values may be sent and summed in bfloat16 or wider, within the bound.
A program may use at most 128 MiB of HBM per device.

v0:
```python
import math

import jax
import jax.numpy as jnp
from jax import lax
from jax.sharding import PartitionSpec as P

HIGHEST = lax.Precision.HIGHEST


def entering(part, axis, combine, identity):
    place = lax.axis_index(axis)
    gathered = jax.tree.map(lambda a: lax.all_gather(a, axis), part)
    state = jax.tree.map(lambda a, e: jnp.zeros_like(a) + jnp.asarray(e, a.dtype), part, identity)

    def one(hop, state):
        return combine(
            state, jax.tree.map(lambda a: lax.dynamic_index_in_dim(a, hop, 0, False), gathered)
        )

    return lax.fori_loop(0, place, one, state)


def from_behind(block, axis, distance):
    devices = range(lax.axis_size(axis))
    route = [((i - distance) % len(devices), i) for i in devices]
    return lax.ppermute(block, axis, route)


def extended_2(block, sides, width):
    for axis, dim in sides:
        count = lax.axis_size(axis)
        forward = [(i, i + 1) for i in range(count - 1)]
        backward = [(target, source) for source, target in forward]
        low = lax.ppermute(
            lax.slice_in_dim(block, block.shape[dim] - width, None, axis=dim), axis, forward
        )
        high = lax.ppermute(lax.slice_in_dim(block, 0, width, axis=dim), axis, backward)
        block = jnp.concatenate([low, block, high], axis=dim)
    return block


def dft_tables(length):
    bin_count = length // 2
    sample = jnp.arange(length, dtype=jnp.int32)
    frequency = jnp.arange(bin_count, dtype=jnp.int32)
    phase_index = sample[:, None] * frequency[None, :] % length
    angle_value = phase_index.astype(jnp.float32) * (2.0 * math.pi / length)
    weights = jnp.where(frequency == 0, 1.0 / length, 2.0 / length).astype(jnp.float32)
    return (jnp.cos(angle_value), jnp.sin(angle_value), weights)


def combine_decay(earlier_map, later_map):
    return (earlier_map[0] * later_map[0], later_map[0] * earlier_map[1] + later_map[1])


def toeplitz_basis(context, taps_bank):
    row_count, context_len = context.shape
    piece_len = context_len // 3
    frame_len = min(128, piece_len)
    basis_num, tap_count = taps_bank.shape
    lag_count = tap_count // frame_len + 1
    line_len = tap_count + 2 * frame_len
    spread = jnp.concatenate(
        [
            jnp.zeros((basis_num, frame_len), taps_bank.dtype),
            taps_bank,
            jnp.zeros((basis_num, frame_len + 1), taps_bank.dtype),
        ],
        axis=1,
    )
    tiled = jnp.tile(spread, (1, frame_len))[:, : frame_len * line_len]
    shifted = tiled.reshape(basis_num, frame_len, line_len)
    table = shifted[:, :, frame_len : frame_len + lag_count * frame_len].reshape(
        basis_num, frame_len, lag_count, frame_len
    )
    first_out = 2 * piece_len // frame_len
    out_frames = piece_len // frame_len
    framed = context.reshape(row_count, context_len // frame_len, frame_len)
    stacked = jnp.stack(
        [framed[:, first_out - lag : first_out - lag + out_frames, :] for lag in range(lag_count)],
        axis=1,
    )
    outputs = jnp.einsum("brfm,imrq->bifq", stacked, table, preferred_element_type=jnp.float32)
    return outputs.reshape(row_count, basis_num, piece_len)


def band_matrix(series, window):
    lead_shape = series.shape[:-1]
    padded = jnp.concatenate([series, jnp.zeros(lead_shape + (window,), series.dtype)], axis=-1)
    tiled = jnp.tile(padded, (1,) * len(lead_shape) + (window,))[..., : window * 3 * window]
    return tiled.reshape(lead_shape + (window, 3 * window))


def chi_square(extended, autocorrelation, window):
    bank_count = extended.shape[0]
    item_count = extended.shape[1]
    total_len = extended.shape[3]
    piece_len = total_len - 2 * window
    frames = piece_len // window
    framed = extended.reshape(bank_count, item_count, 2, frames + 2, window)
    triple = jnp.concatenate(
        [framed[..., 0:frames, :], framed[..., 1 : frames + 1, :], framed[..., 2 : frames + 2, :]],
        axis=-1,
    )
    band_mats = band_matrix(autocorrelation, window)
    folded = jnp.einsum("bmpnk,bdqk->bmpdnq", triple, band_mats, precision=HIGHEST)
    corr_real = folded[:, :, 0, 0] + folded[:, :, 1, 1]
    corr_imag = folded[:, :, 1, 0] - folded[:, :, 0, 1]
    power_ext = extended[:, :, 0] * extended[:, :, 0] + extended[:, :, 1] * extended[:, :, 1]
    power_framed = power_ext.reshape(bank_count, item_count, frames + 2, window)
    power_triple = jnp.concatenate(
        [
            power_framed[..., 0:frames, :],
            power_framed[..., 1 : frames + 1, :],
            power_framed[..., 2 : frames + 2, :],
        ],
        axis=-1,
    )
    ones_band = band_matrix(jnp.ones((1, 2 * window + 1), jnp.float32), window)[0]
    window_sum = jnp.einsum("bmnk,qk->bmnq", power_triple, ones_band, precision=HIGHEST)
    centre = extended[..., window : window + piece_len].reshape(
        bank_count, item_count, 2, frames, window
    )
    energy = centre[:, :, 0] * centre[:, :, 0] + centre[:, :, 1] * centre[:, :, 1]
    lag_energy = jnp.sum(autocorrelation * autocorrelation, axis=(1, 2))
    cross = centre[:, :, 0] * corr_real + centre[:, :, 1] * corr_imag
    chisq = (window_sum - 2.0 * cross + energy * lag_energy[:, None, None, None]) / (2 * window + 1)
    return (
        energy.reshape(bank_count, item_count, piece_len),
        chisq.reshape(bank_count, item_count, piece_len),
    )


def body(
    strain, gate_mask, psd_reset, psd_ref, psd_rate, filters, basis_count, mixing, autocorrelation
):
    piece_len = strain.shape[1]
    cos_table, sin_table, weights = dft_tables(piece_len)
    signal = strain[0] * gate_mask.astype(jnp.float32)
    real_part = jnp.dot(signal, cos_table, precision=HIGHEST)
    imag_part = jnp.dot(signal, sin_table, precision=HIGHEST)
    reference_psd = psd_ref[0]
    decay_rate = psd_rate[0]
    log_power = jnp.log(
        (real_part * real_part + imag_part * imag_part) / (piece_len / 2) + 0.1 * reference_psd
    )
    keep_factor = (1.0 - decay_rate) * (1.0 - 0.5 * psd_reset[0].astype(jnp.float32))
    drive_term = decay_rate * log_power
    prior_keep, prior_drive = entering(
        (keep_factor, drive_term),
        ("bank", "tm"),
        combine_decay,
        (jnp.ones_like(keep_factor), jnp.zeros_like(drive_term)),
    )
    log_psd = keep_factor * (prior_keep * jnp.log(reference_psd) + prior_drive) + drive_term
    bin_scale = jnp.exp(-0.5 * log_psd) * weights
    whitened = jnp.dot(cos_table, real_part * bin_scale, precision=HIGHEST) + jnp.dot(
        sin_table, imag_part * bin_scale, precision=HIGHEST
    )
    own_row = whitened.astype(jnp.bfloat16).reshape(1, piece_len)
    gathered = lax.all_gather(own_row, "bank", axis=0, tiled=True)
    at_start = lax.axis_index("tm") == 0
    earlier = gathered
    previous = []
    for hop_count in range(2):
        moved_rows = from_behind(earlier, "tm", 1)
        rolled = jnp.concatenate([jnp.zeros_like(moved_rows[:1]), moved_rows[:-1]], axis=0)
        earlier = jnp.where(at_start, rolled, moved_rows)
        previous.append(earlier)
    context = jnp.concatenate([previous[1], previous[0], gathered], axis=1)
    basis_out = toeplitz_basis(context, filters[0, 0])
    live_basis = (jnp.arange(basis_out.shape[1], dtype=jnp.int32) < basis_count[0]).astype(
        jnp.float32
    )
    basis_rounded = (basis_out * live_basis[None, :, None]).astype(jnp.bfloat16)
    mixing_local = mixing[0, 0]
    templ_total = mixing_local.shape[0]
    share_count = templ_total // lax.axis_size("rate")
    window = autocorrelation.shape[2] // 2
    all_basis, all_mixing = (
        lax.all_gather(basis_rounded[None], "rate", axis=0, tiled=True),
        lax.all_gather(mixing, "rate", axis=1, tiled=True),
    )
    row_start = lax.axis_index("rate") * share_count
    own_mixing = lax.dynamic_slice_in_dim(all_mixing[0], row_start, share_count, 1)
    snr_part = jnp.einsum(
        "cmpi,cbit->mpbt", own_mixing, all_basis, preferred_element_type=jnp.float32
    )
    received = lax.all_to_all(snr_part[None], "bank", split_axis=3, concat_axis=0, tiled=True)
    shaped = received.reshape(received.shape[0], received.shape[1], 2, received.shape[4])
    extended = extended_2(shaped, ((("bank", "tm"), 3),), window)
    snr_sq, chisq = chi_square(extended, autocorrelation, window)
    return (snr_sq, chisq)


def solution(mesh):
    return jax.shard_map(
        body,
        mesh=mesh,
        in_specs=(
            P("rate", ("parts", "bank", "tm")),
            P(("parts", "bank", "tm")),
            P(("parts", "bank", "tm")),
            P("rate", None),
            P("rate", None),
            P("bank", "rate", None, None),
            P("bank"),
            P("bank", "rate", None, None, None),
            P(),
        ),
        out_specs=(
            P(None, "rate", ("parts", "bank", "tm")),
            P(None, "rate", ("parts", "bank", "tm")),
        ),
        check_vma=False,
    )
```

profile of v0, /device:TPU:0, one launch (start us, length us, event | category | flops | bytes accessed | tf_op | source)
XLA Modules:
  0.0 247.6 jit_solution(3940699285153602173)
XLA Ops:
  0.6 0.7 convert_multiply_fusion
  1.3 8.7 %fusion.17 = f32[1,512]{1,0:T(1,128)S(1)} fusion(f32[1024,1]{0,1:T(1,128)S(1)} %bitcast.279), kind=kOutput, calls=%fused_computation.23 | convolution fusion | flops 13631488 | bytes 6144 | tf_op jit(solution)/shard_map/dot_general | solution.py:141
  10.0 0.0 copy-start.4
  10.0 0.0 copy-start.2
  10.1 8.8 %fusion.21 = f32[1,512]{1,0:T(1,128)S(1)} fusion(f32[1024,1]{0,1:T(1,128)S(1)} %bitcast.280), kind=kOutput, calls=%fused_computation.25 | convolution fusion | flops 13631488 | bytes 6144 | tf_op jit(solution)/shard_map/dot_general | solution.py:142
  18.8 0.0 copy-done.4
  19.5 0.0 copy-done.2
  19.6 27.8 %all-gather.2 = f32[8,1,512]{2,1,0:T(1,128)S(1)} all-gather(f32[1,1,512]{2,1,0:T(1,128)S(1)} %multiply_bitcast_fusion), channel_id=1, replica_groups=mesh['parts'=2,'bank'=4,'tm'=2,'rate'=2] {'bank','tm'}, dimensions={0}, use_global_device_ids=true | all-gather | bytes 18432 | tf_op jit(solution)/shard_map/all_gather | solution.py:13
  47.4 26.0 %all-gather.3 = f32[8,1,512]{2,1,0:T(1,128)S(1)} all-gather(f32[1,1,512]{2,1,0:T(1,128)S(1)} %bitcast.269), channel_id=2, replica_groups=mesh['parts'=2,'bank'=4,'tm'=2,'rate'=2] {'bank','tm'}, dimensions={0}, use_global_device_ids=true | all-gather | bytes 18432 | tf_op jit(solution)/shard_map/all_gather | solution.py:13
  73.4 0.2 while.12
  73.6 10.4 %fusion.15 = f32[1,1024]{1,0:T(1,128)S(1)} fusion(f32[512,1]{0,1:T(1,128)S(1)} %bitcast.284), kind=kOutput, calls=%fused_computation.22 | convolution fusion | flops 13631488 | bytes 6144 | tf_op jit(solution)/shard_map/dot_general | solution.py:158
  84.0 0.0 copy-start.5
  84.0 0.0 copy-start.3
  84.0 0.0 copy-start
  84.0 10.4 %fusion.19 = f32[1,1024]{1,0:T(1,128)S(1)} fusion(f32[512,1]{0,1:T(1,128)S(1)} %bitcast.283), kind=kOutput, calls=%fused_computation.24 | convolution fusion | flops 13631488 | bytes 6144 | tf_op jit(solution)/shard_map/dot_general | solution.py:158
  94.4 11.9 %all-gather.1 = bf16[4096]{0:T(1024)(128)(2,1)S(1)} all-gather(bf16[1024]{0:T(1024)(128)(2,1)S(1)} %add_convert_fusion), channel_id=3, replica_groups=mesh['parts'=2,'bank'=4,'tm'=2,'rate'=2] {'bank'}, dimensions={0}, use_global_device_ids=true | all-gather | bytes 10240 | tf_op jit(solution)/shard_map/all_gather | solution.py:162
  106.3 0.1 collective-permute-start
  106.5 0.0 copy-done.5
  106.5 1.8 all_gather.19
  108.3 0.0 copy-done.3
  108.3 0.5 tile.29
  108.8 0.5 slice_reduce_fusion
  109.3 0.0 copy-done
  110.1 0.0 collective-permute-done
  110.1 2.0 collective-permute-start.1
  112.1 6.9 %tile.12 = bf16[32,128,2305]{2,1,0:T(8,128)(2,1)} broadcast(bf16[32,2305]{1,0:T(8,128)(2,1)S(1)} %maximum_maximum_fusion), dimensions={0,2} | broadcast | bytes 19030080 | tf_op jit(solution)/shard_map/tile | solution.py:72
  119.0 44.8 %tile.13 = bf16[32,295040]{1,0:T(8,128)(2,1)} reshape(bf16[32,128,2305]{2,1,0:T(8,128)(2,1)} %tile.12) | data formatting | bytes 37765120 | tf_op jit(solution)/shard_map/tile | solution.py:72
  163.8 0.0 slice-start
  163.8 6.4 %slice-done = bf16[32,294912]{1,0:T(8,128)(2,1)S(1)} async-done(((bf16[32,295040]{1,0:T(8,128)(2,1)}), bf16[32,294912]{1,0:T(8,128)(2,1)S(1)}, s32[]{:S(2)}) %slice-start) | async-done | bytes 18874392 | tf_op jit(solution)/shard_map/slice | solution.py:72
  170.2 9.7 %copy.103 = bf16[4,8,128,2304]{3,2,1,0:T(8,128)(2,1)S(1)} copy(bf16[4,8,128,2304]{3,1,2,0:T(8,128)(2,1)S(1)} %bitcast.240) | data formatting | bytes 37748736
  179.8 7.0 %slice.163 = bf16[32,128,2176]{2,1,0:T(8,128)(2,1)} slice(bf16[32,128,2304]{2,1,0:T(8,128)(2,1)S(1)} %bitcast.241), slice={[0:32], [0:128], [128:2304]} | slice | bytes 35651584 | tf_op jit(solution)/shard_map/slice | solution.py:74
  186.9 0.0 copy-start.1
  186.9 22.1 %copy.100 = bf16[32,128,2176]{1,2,0:T(8,128)(2,1)} copy(bf16[32,128,2176]{2,1,0:T(8,128)(2,1)} %slice.163) | data formatting | bytes 35651584
  209.0 0.0 copy-done.1
  209.0 0.3 tile.30
  209.3 3.6 %tile.31 = f32[4,2,49280]{2,1,0:T(2,128)} reshape(f32[4,2,128,385]{3,2,1,0:T(8,128)S(1)} %tile.30) | data formatting | bytes 3153920 | tf_op jit(solution)/shard_map/tile | solution.py:91
  212.8 0.0 slice-start.1
  212.8 1.4 slice-done.1
  214.3 1.4 reshape.119
  215.6 0.0 collective-permute-done.1
  216.0 8.8 %convolution_bitcast_fusion = f32[4,32,8,128]{3,2,0,1:T(8,128)S(1)} fusion(bf16[32,128,17,128,1]{1,3,2,4,0:T(8,128)(2,1)} %bitcast.239, bf16[4,17,8,128]{3,2,1,0:T(8,128)(2,1)S(1)} %constant_dynamic-update-slice_fusion), kind=kOutput, calls=%fused_computation.14 | convolution fusion | flops 570425344 | bytes 18489344 | tf_op jit(solution)/shard_map/brfm,imrq->bifq/dot_general | solution.py:84
  224.8 0.2 reshape.92
  225.0 0.3 fusion.24
  225.3 2.2 all_gather.24
  227.5 0.3 convolution_bitcast_fusion.1
  227.8 0.6 copy.84
  228.4 3.3 %all-to-all-start = ((f32[1,2,2,4,1024]{4,2,1,0,3:T(2,128)}), f32[1,2,2,4,1024]{4,2,1,0,3:T(2,128)S(1)}, u32[]{:S(2)}, u32[]{:S(2)}) async-start(f32[1,2,2,4,1024]{4,2,1,0,3:T(2,128)} %copy.84), calls=%async_computation | async-start | bytes 131072 | tf_op jit(solution)/shard_map/all_to_all | solution.py:190
  231.7 0.1 multiply_reduce_fusion
  231.8 5.6 %all-to-all-done = f32[1,2,2,4,1024]{4,2,1,0,3:T(2,128)S(1)} async-done(((f32[1,2,2,4,1024]{4,2,1,0,3:T(2,128)}), f32[1,2,2,4,1024]{4,2,1,0,3:T(2,128)S(1)}, u32[]{:S(2)}, u32[]{:S(2)}) %all-to-all-start) | async-done | bytes 65568 | tf_op jit(solution)/shard_map/all_to_all | solution.py:190
  237.4 0.1 reshape.121
  237.5 1.3 collective-permute-start.3
  238.8 4.5 %collective-permute-start.2 = (f32[4,2,2,128]{3,2,1,0:T(2,128)S(1)}, f32[4,2,2,128]{3,2,1,0:T(2,128)S(1)}, u32[]{:S(2)}, u32[]{:S(2)}) collective-permute-start(f32[4,2,2,128]{3,2,1,0:T(2,128)S(1)} %get-tuple-element.62), channel_id=1, source_target_pairs={{0,2},{2,4},{4,6},{6,8},{8,10},{10,12},{12,14},{1,3},{3,5},{5,7},{... | collective-permute-start | bytes 24584 | tf_op jit(solution)/shard_map/ppermute | solution.py:35
  243.3 0.6 add.87
  244.0 0.0 collective-permute-done.3
  244.0 0.7 collective-permute-done.2
  244.7 0.2 fusion.34
  244.9 0.1 reshape.95
  245.0 1.6 fusion.8
  246.6 0.4 fusion.12
  247.0 0.6 reshape.96
  (49 shorter events, 0.6 us)
Async XLA Ops:
  10.0 8.8 %copy-start.4 = (f32[1,512]{1,0:T(1,128)S(1)}, f32[1,512]{1,0:T(1,128)}, u32[]{:S(2)}) copy-start(f32[1,512]{1,0:T(1,128)} %param.14) | copy-start | bytes 6148
  10.0 9.5 %copy-start.2 = (f32[1,512]{1,0:T(1,128)S(1)}, f32[1,512]{1,0:T(1,128)}, u32[]{:S(2)}) copy-start(f32[1,512]{1,0:T(1,128)} %param.15) | copy-start | bytes 6148
  84.0 22.5 %copy-start.5 = (bf16[1,1,4,2,32]{4,3,2,1,0:T(2,128)(2,1)S(1)}, bf16[1,1,4,2,32]{4,3,2,1,0:T(2,128)(2,1)}, u32[]{:S(2)}) copy-start(bf16[1,1,4,2,32]{4,3,2,1,0:T(2,128)(2,1)} %param.18) | copy-start | bytes 1540
  84.0 24.3 %copy-start.3 = (f32[385]{0:T(512)S(1)}, f32[385]{0:T(512)}, u32[]{:S(2)}) copy-start(f32[385]{0:T(512)} %constant.76.clone.1) | copy-start | bytes 4624
  84.0 25.3 %copy-start = (bf16[1,1,32,2048]{3,2,1,0:T(8,128)(2,1)S(1)}, bf16[1,1,32,2048]{3,2,1,0:T(8,128)(2,1)}, u32[]{:S(2)}) copy-start(bf16[1,1,32,2048]{3,2,1,0:T(8,128)(2,1)} %param.16) | copy-start | bytes 393220
  106.3 3.8 %collective-permute-start = (bf16[4,1024]{1,0:T(4,128)(2,1)S(1)}, bf16[4,1024]{1,0:T(4,128)(2,1)S(1)}, u32[]{:S(2)}, u32[]{:S(2)}) collective-permute-start(bf16[4,1024]{1,0:T(4,128)(2,1)S(1)} %reshape.98), channel_id=1, source_target_pairs={{2,0},{0,2},{3,1},{1,3},{6,4},{4,6},{7,5},{5,7},{10,8},{8,10},{11,... | collective-permute-start | bytes 24584 | tf_op jit(solution)/shard_map/ppermute | solution.py:27
  110.1 105.6 %collective-permute-start.1 = (bf16[4,1024]{1,0:T(4,128)(2,1)S(1)}, bf16[4,1024]{1,0:T(4,128)(2,1)S(1)}, u32[]{:S(2)}, u32[]{:S(2)}) collective-permute-start(bf16[4,1024]{1,0:T(4,128)(2,1)S(1)} %pad_select_fusion.1), channel_id=1, source_target_pairs={{2,0},{0,2},{3,1},{1,3},{6,4},{4,6},{7,5},{5,7},{10,8},{8,10},{11,... | collective-permute-start | bytes 24584 | tf_op jit(solution)/shard_map/ppermute | solution.py:27
  163.8 6.4 %slice-start = ((bf16[32,295040]{1,0:T(8,128)(2,1)}), bf16[32,294912]{1,0:T(8,128)(2,1)S(1)}, s32[]{:S(2)}) async-start(bf16[32,295040]{1,0:T(8,128)(2,1)} %tile.13), calls=%async_computation.1 | async-start | bytes 37748736 | tf_op jit(solution)/shard_map/slice | solution.py:72
  186.9 22.1 %copy-start.1 = (f32[4,2,257]{2,1,0:T(2,128)S(1)}, f32[4,2,257]{2,1,0:T(2,128)}, u32[]{:S(2)}) copy-start(f32[4,2,257]{2,1,0:T(2,128)} %param.19) | copy-start | bytes 24676
  212.8 1.4 slice-start.1
  228.4 9.0 %all-to-all-start = ((f32[1,2,2,4,1024]{4,2,1,0,3:T(2,128)}), f32[1,2,2,4,1024]{4,2,1,0,3:T(2,128)S(1)}, u32[]{:S(2)}, u32[]{:S(2)}) async-start(f32[1,2,2,4,1024]{4,2,1,0,3:T(2,128)} %copy.84), calls=%async_computation | async-start | bytes 131072 | tf_op jit(solution)/shard_map/all_to_all | solution.py:190
  237.5 6.5 %collective-permute-start.3 = (f32[4,2,2,128]{3,2,1,0:T(2,128)S(1)}, f32[4,2,2,128]{3,2,1,0:T(2,128)S(1)}, u32[]{:S(2)}, u32[]{:S(2)}) collective-permute-start(f32[4,2,2,128]{3,2,1,0:T(2,128)S(1)} %get-tuple-element.63), channel_id=1, source_target_pairs={{2,0},{4,2},{6,4},{8,6},{10,8},{12,10},{14,12},{3,1},{5,3},{7,5},{... | collective-permute-start | bytes 24584 | tf_op jit(solution)/shard_map/ppermute | solution.py:38
  238.8 5.9 %collective-permute-start.2 = (f32[4,2,2,128]{3,2,1,0:T(2,128)S(1)}, f32[4,2,2,128]{3,2,1,0:T(2,128)S(1)}, u32[]{:S(2)}, u32[]{:S(2)}) collective-permute-start(f32[4,2,2,128]{3,2,1,0:T(2,128)S(1)} %get-tuple-element.62), channel_id=1, source_target_pairs={{0,2},{2,4},{4,6},{6,8},{8,10},{10,12},{12,14},{1,3},{3,5},{5,7},{... | collective-permute-start | bytes 24584 | tf_op jit(solution)/shard_map/ppermute | solution.py:35
where the time goes:
time: 249 us; the launch traced here: 248 us
  local copies, waits for them, and re-layouts  107 us (43%)
  blocking collectives  69.6 us (28%)
  matrix products  49.3 us (20%)
  starting transfers between devices  11.3 us (5%)
  waiting for transfers between devices  6.3 us (3%)
    all_gather x2, blocking collectives, entering(): gathered = jax.tree.map(lambda a: lax.all_gather(a, axis), part)  53.8 us
    another operation x2, local copies, waits for them, and re-layouts, toeplitz_basis(): tiled = jnp.tile(spread, (1, frame_len))[:, :frame_len * line_len]  51.7 us
    unnamed x34, local copies, waits for them, and re-layouts  32 us
    all_gather x1, blocking collectives, body(): gathered = lax.all_gather(own_row, 'bank', axis=0, tiled=True)  11.9 us
    dot_general x1, matrix products, body(): jnp.dot(sin_table, imag_part * bin_scale, precision=HIGHEST)  10.4 us
    dot_general x1, matrix products, body(): jnp.dot(cos_table, real_part * bin_scale, precision=HIGHEST)  10.4 us
    dot_general x1, matrix products, toeplitz_basis(): jnp.einsum('brfm,imrq->bifq', stacked, table, preferred_element_type=jnp....  8.84 us
    dot_general x1, matrix products, body(): imag_part = jnp.dot(signal, sin_table, precision=HIGHEST)  8.79 us
  transfers between devices with their start and end apart: 5, of which 2 were waited for; matrix products, arithmetic and copies ran while one was open for 39% of the time, Pallas kernels for 0%

commit v1 on v0

v1 whole, which is shorter than its diff:
```python
import functools
import math

import jax
import jax.numpy as jnp
import numpy as np
from jax import lax
from jax.experimental import pallas as pl
from jax.experimental.pallas import tpu as pltpu
from jax.sharding import PartitionSpec as P

HIGHEST = lax.Precision.HIGHEST
F32 = jnp.float32
BF16 = jnp.bfloat16
LANES = 128
MESH = pl.DeviceIdType.MESH


def dft_constants(length, group):
    rows = length // LANES
    half = length // 2 // rows
    n1 = np.arange(rows)
    n2 = np.arange(LANES)
    small = 2.0 * np.pi * ((n1[:, None] * n1[None, :]) % rows) / rows
    eye = np.eye(group)
    first = np.concatenate([np.kron(eye, np.cos(small)), np.kron(eye, np.sin(small))], axis=0)
    last = np.concatenate([np.kron(eye, np.cos(small)), np.kron(eye, np.sin(small))], axis=1)
    angle = 2.0 * np.pi * (n1[:, None] * n2[None, :]) / length
    twiddle = np.stack([np.cos(angle), np.sin(angle)])
    wide = 2.0 * np.pi * ((n2[:, None] * n2[None, :]) % LANES) / LANES
    live = (n2 < half).astype(np.float64)
    c, s = np.cos(wide) * live, np.sin(wide) * live
    forward = np.concatenate(
        [np.concatenate([c, s], axis=1), np.concatenate([-s, c], axis=1)], axis=0
    )
    ct, st = c.T, s.T
    inverse = np.concatenate(
        [np.concatenate([ct, -st], axis=1), np.concatenate([st, ct], axis=1)], axis=0
    )
    return tuple(a.astype(np.float32) for a in (first, twiddle, forward, inverse, last))


def iota(shape, dim):
    return lax.broadcasted_iota(jnp.int32, shape, dim)


def each(count, step):
    if count <= 32:
        for i in range(count):
            step(i)
    else:
        lax.fori_loop(0, count, lambda i, c: (step(i), c)[1], 0)


def split(x):
    high = x.astype(BF16)
    return high, (x - high.astype(F32)).astype(BF16)


def nt_dot(a, b):
    return lax.dot_general(a, b, (((1,), (1,)), ((), ())), preferred_element_type=F32)


def kernel(
    sizes,
    strain,
    gate,
    reset,
    ref,
    rate,
    filters,
    count,
    mixing,
    auto,
    first,
    twiddle,
    forward,
    inverse,
    last,
    out_sq,
    out_chi,
    xbuf,
    pbuf,
    gsend,
    gbuf,
    wbuf,
    lbuf,
    yre,
    yim,
    rpad,
    rhi,
    rlo,
    x_send,
    x_recv,
    p_send,
    p_recv,
    g_send,
    g_recv,
):
    nb, ntm, nr, group = sizes
    nblk = nb * ntm
    slots = nr * nblk
    rows = xbuf.shape[1] // 2
    taps = filters.shape[1]
    lags = taps // LANES
    bank, tm, core = lax.axis_index("bank"), lax.axis_index("tm"), lax.axis_index("rate")
    block = bank * ntm + tm
    me = core * nblk + block

    def device(slot):
        blk = lax.rem(slot, nblk)
        return {"bank": blk // ntm, "tm": lax.rem(blk, ntm), "rate": slot // nblk}

    barrier = pltpu.get_barrier_semaphore()

    def greet(i):
        pl.semaphore_signal(
            barrier, inc=1, device_id=device(lax.rem(me + i + 1, slots)), device_id_type=MESH
        )

    each(slots - 1, greet)

    xbuf[me, 0:rows, :] = strain[...] * gate[...].astype(F32)
    xbuf[me, rows : 2 * rows, :] = jnp.full((rows, LANES), reset[0], jnp.int32).astype(F32)
    bin_rows = ref.shape[0]
    pbuf[core, 0:bin_rows, :] = ref[...]
    pbuf[core, bin_rows : 2 * bin_rows, :] = rate[...]

    pl.semaphore_wait(barrier, slots - 1)

    def x_copy(src_slot, target, i):
        return pltpu.make_async_remote_copy(
            src_ref=xbuf.at[src_slot],
            dst_ref=xbuf.at[src_slot],
            send_sem=x_send.at[i],
            recv_sem=x_recv.at[src_slot],
            device_id=device(target),
            device_id_type=MESH,
        )

    def p_copy(src_core, target, i):
        return pltpu.make_async_remote_copy(
            src_ref=pbuf.at[src_core],
            dst_ref=pbuf.at[src_core],
            send_sem=p_send.at[i],
            recv_sem=p_recv.at[src_core],
            device_id={"rate": target},
            device_id_type=MESH,
        )

    each(slots - 1, lambda i: x_copy(me, lax.rem(me + i + 1, slots), i).start())
    for i in range(nr - 1):
        p_copy(core, lax.rem(core + i + 1, nr), i).start()

    basis = filters.shape[0]
    mix_rows = mixing.shape[0]
    share = mix_rows // nr // 2
    live = (iota((mix_rows, basis), 1) < count[0]).astype(F32)
    dest, source = iota((mix_rows, mix_rows), 0), iota((mix_rows, mix_rows), 1)
    inner = dest % (2 * share)
    wanted = dest // (2 * share) * (2 * share) + inner % share * 2 + inner // share
    perm = (source == wanted).astype(F32)
    mixed_rows = jnp.dot(perm, mixing[...].astype(F32) * live, preferred_element_type=F32)
    mixed = jnp.dot(mixed_rows.astype(BF16), filters[...], preferred_element_type=F32)
    upper = iota((8, LANES), 0) < 4
    for r in range(nr):
        for quad in range(lags // 4):
            parts = []
            for h in range(2):
                at = (4 * quad + 2 * h) * LANES
                low, high = mixed[:, at : at + LANES], mixed[:, at + LANES : at + 2 * LANES]
                if r == 0:
                    high = pltpu.roll(high, 4, 0)
                else:
                    low = pltpu.roll(low, 4, 0)
                parts.append(jnp.where(upper, low, high))
            gsend[r, quad] = jnp.concatenate(parts, axis=0).astype(BF16)

    peers = nb * nr
    mine = core * nb + bank

    def g_copy(source, target, i):
        return pltpu.make_async_remote_copy(
            src_ref=gsend.at[target // nb],
            dst_ref=gbuf.at[source // nb, :, lax.rem(source, nb)],
            send_sem=g_send.at[i],
            recv_sem=g_recv.at[source],
            device_id={"bank": lax.rem(target, nb), "rate": target // nb},
            device_id_type=MESH,
        )

    each(peers - 1, lambda i: g_copy(mine, lax.rem(mine + i + 1, peers), i).start())
    gbuf[core, :, bank] = gsend[core]

    window = auto.shape[2] // 2
    span = 3 * LANES
    rpad[...] = jnp.zeros_like(rpad)
    for b in range(nb):
        for d in range(2):
            rpad[2 * b + d : 2 * b + d + 1, 0 : auto.shape[2]] = auto[b, d : d + 1, :]
    lag_energy = []
    for b in range(nb):
        series = rpad[2 * b : 2 * b + 2, :]
        lag_energy.append(jnp.sum(series * series, keepdims=True))

    def band(row):
        line = jnp.broadcast_to(rpad[pl.ds(row, 1), :], (LANES, span))
        high, low = split(pltpu.roll(line, 0, 1, stride=1, stride_axis=0))
        rhi[row] = high
        rlo[row] = low

    each(2 * nb, band)
    offset = iota((LANES, span), 1) - iota((LANES, span), 0)
    ones_band = ((offset >= 0) & (offset <= 2 * window)).astype(F32).astype(BF16)

    for i in range(nr - 1):
        p_copy(lax.rem(core + i + 1, nr), core, i).wait_recv()
    each(slots - 1, lambda i: x_copy(lax.rem(me + i + 1, slots), me, i).wait_recv())

    bins = bin_rows * LANES
    pick = iota((rows, LANES), 1) % rows == iota((rows, LANES), 0)
    lines = []
    for c in range(nr):
        for which in range(2):
            pieces = []
            for q in range(bin_rows):
                row = pbuf[c, which * bin_rows + q : which * bin_rows + q + 1, :]
                pieces.append(jnp.where(pick, jnp.broadcast_to(row, (rows, LANES)), 0.0))
            lines.append(jnp.concatenate(pieces, axis=1))
    gather = (iota((bins, LANES), 0) // rows == iota((bins, LANES), 1)).astype(F32)
    psd = jnp.dot(
        jnp.concatenate(lines, axis=0), gather, precision=HIGHEST, preferred_element_type=F32
    )
    lane = iota((rows, LANES), 1)
    live_bin = lane < bins // rows
    length = rows * LANES
    weight = jnp.where(
        live_bin,
        jnp.where((lane == 0) & (iota((rows, LANES), 0) == 0), 1.0 / length, 2.0 / length),
        0.0,
    )
    refs = [jnp.where(live_bin, psd[2 * c * rows : (2 * c + 1) * rows], 1.0) for c in range(nr)]
    rates = [psd[(2 * c + 1) * rows : (2 * c + 2) * rows] for c in range(nr)]

    tall = group * rows
    cos_tw = jnp.broadcast_to(twiddle[0][None], (group, rows, LANES)).reshape(tall, LANES)
    sin_tw = jnp.broadcast_to(twiddle[1][None], (group, rows, LANES)).reshape(tall, LANES)
    for s in range(slots // group):
        x = xbuf[s * group : (s + 1) * group, 0:rows, :].reshape(tall, LANES)
        y = jnp.dot(first[...], x, precision=HIGHEST, preferred_element_type=F32)
        a, b = y[:tall], y[tall:]
        turned = jnp.concatenate([a * cos_tw - b * sin_tw, a * sin_tw + b * cos_tw], axis=1)
        spec = jnp.dot(turned, forward[...], precision=HIGHEST, preferred_element_type=F32)
        real, imag = spec[:, :LANES], spec[:, LANES:]
        yre[s * group : (s + 1) * group] = real.reshape(group, rows, LANES)
        yim[s * group : (s + 1) * group] = imag.reshape(group, rows, LANES)
        power = (real * real + imag * imag) / (length / 2)
        lbuf[s * group : (s + 1) * group] = power.reshape(group, rows, LANES)

    def advance(i, states):
        after = []
        for c in range(nr):
            at = c * nblk + i
            keep = (1.0 - rates[c]) * (1.0 - 0.5 * xbuf[at, rows : 2 * rows, :])
            level = jnp.log(lbuf[at] + 0.1 * refs[c])
            state = keep * states[c] + rates[c] * level
            lbuf[at] = jnp.exp(-0.5 * state) * weight
            after.append(state)
        return tuple(after)

    states = tuple(jnp.log(refs[c]) for c in range(nr))
    if nblk <= 16:
        for i in range(nblk):
            states = advance(i, states)
    else:
        lax.fori_loop(0, nblk, advance, states)

    pad = wbuf.shape[1] - nblk * rows - rows
    for c in range(nr):
        wbuf[c, 0:pad, :] = jnp.zeros((pad, LANES), F32)
        wbuf[c, pad + nblk * rows :, :] = jnp.zeros((rows, LANES), F32)
    per_copy = min(group, nblk)
    for s in range(slots // group):
        scale = lbuf[s * group : (s + 1) * group].reshape(tall, LANES)
        real = yre[s * group : (s + 1) * group].reshape(tall, LANES) * scale
        imag = yim[s * group : (s + 1) * group].reshape(tall, LANES) * scale
        y = jnp.dot(
            jnp.concatenate([real, imag], axis=1),
            inverse[...],
            precision=HIGHEST,
            preferred_element_type=F32,
        )
        a, b = y[:, :LANES], y[:, LANES:]
        turned = jnp.concatenate([a * cos_tw + b * sin_tw, b * cos_tw - a * sin_tw], axis=0)
        white = jnp.dot(last[...], turned, precision=HIGHEST, preferred_element_type=F32)
        white = white.astype(BF16).astype(F32)
        for piece in range(group // per_copy):
            slot = s * group + piece * per_copy
            c, blk = slot // nblk, slot % nblk
            at = pad + blk * rows
            wbuf[c, at : at + per_copy * rows, :] = white[
                piece * per_copy * rows : (piece + 1) * per_copy * rows
            ]

    each(peers - 1, lambda i: g_copy(lax.rem(mine + i + 1, peers), mine, i).wait_recv())
    frames = rows + 2
    start = pl.multiple_of(block * rows, rows)
    view = [wbuf[c, pl.ds(start, pad + 2 * rows), :] for c in range(nr)]
    quads = lags // 4
    table = jnp.concatenate(
        [gbuf[c].reshape(quads * nb * 16, LANES) for c in range(nr)], axis=1
    )
    later = iota((LANES, LANES), 1) >= iota((LANES, LANES), 0)

    def spun(c, row):
        line = jnp.broadcast_to(view[c][row : row + 1, :], (LANES, LANES))
        return pltpu.roll(line, 0, 1, stride=1, stride_axis=0)

    total = [None] * (frames + 1)
    before = [spun(c, pad - lags - 1) for c in range(nr)]
    for a in range(frames + lags - 1):
        now = [spun(c, pad - lags + a) for c in range(nr)]
        toeplitz = jnp.concatenate(
            [jnp.where(later, now[c], before[c]).astype(BF16) for c in range(nr)], axis=0
        )
        before = now
        lowest = max(0, -((a - lags + 4) // 4))
        highest = min(quads - 1, (frames - 1 - a + lags - 1) // 4)
        got = jnp.dot(
            table[lowest * nb * 16 : (highest + 1) * nb * 16],
            toeplitz,
            preferred_element_type=F32,
        ).reshape(highest + 1 - lowest, nb, 2, 8, LANES)
        for quad in range(lowest, highest + 1):
            for h in range(2):
                place = a - (lags - 1) + 4 * quad + 2 * h
                if -1 <= place < frames:
                    term = got[quad - lowest, :, h]
                    old = total[place + 1]
                    total[place + 1] = term if old is None else old + term

    inside = (block < nblk - 1).astype(F32)
    pairs = nb // 2
    series = []
    for f in range(frames):
        line = []
        for j in range(pairs):
            both = []
            for b in (2 * j, 2 * j + 1):
                both.append(total[f + 1][b] + pltpu.roll(total[f][b], 4, 0))
            line.append(jnp.where(upper, both[0], pltpu.roll(both[1], 4, 0)))
            if f == frames - 1:
                line[-1] = line[-1] * inside
        series.append(line)

    height = rows * 8
    row = iota((height, LANES), 0)
    even = row % 8 < 4
    first_phase = row % 4 < 2
    for j in range(pairs):
        triple = jnp.concatenate(
            [
                jnp.concatenate([series[f + k][j] for f in range(rows)], axis=0)
                for k in range(3)
            ],
            axis=1,
        )
        centre = triple[:, LANES : 2 * LANES]
        high, low = split(triple)
        stacked = jnp.concatenate([high, low], axis=0)
        upper_table = rhi[4 * j : 4 * j + 4].reshape(4 * LANES, span)
        lower_table = rlo[4 * j : 4 * j + 4].reshape(4 * LANES, span)
        folded = nt_dot(stacked, upper_table)
        folded = folded[:height] + folded[height:] + nt_dot(high, lower_table)
        with_real = jnp.where(even, folded[:, :LANES], folded[:, 2 * LANES : 3 * LANES])
        with_imag = jnp.where(even, folded[:, LANES : 2 * LANES], folded[:, 3 * LANES :])
        corr = with_real + jnp.where(
            first_phase, pltpu.roll(with_imag, height - 2, 0), -pltpu.roll(with_imag, 2, 0)
        )
        square = triple * triple
        summed = nt_dot(jnp.concatenate(split(square), axis=0), ones_band)
        summed = summed[:height] + summed[height:]
        own = centre * centre
        lag = jnp.where(even, lag_energy[2 * j], lag_energy[2 * j + 1])
        value = summed - 2.0 * centre * corr + own * lag
        chi = (value + pltpu.roll(value, height - 2, 0)) / (2 * window + 1)
        energy = own + pltpu.roll(own, height - 2, 0)
        for f in range(rows):
            for half in range(2):
                at = 8 * f + 4 * half
                cols = slice(f * LANES, (f + 1) * LANES)
                out_sq[2 * j + half, :, cols] = energy[at : at + share]
                out_chi[2 * j + half, :, cols] = chi[at : at + share]

    for i in range(nr - 1):
        p_copy(core, lax.rem(core + i + 1, nr), i).wait_send()
    each(slots - 1, lambda i: x_copy(me, lax.rem(me + i + 1, slots), i).wait_send())
    each(peers - 1, lambda i: g_copy(mine, lax.rem(mine + i + 1, peers), i).wait_send())


def body(
    strain, gate_mask, psd_reset, psd_ref, psd_rate, filters, basis_count, mixing, autocorrelation
):
    nb, ntm, nr = lax.axis_size("bank"), lax.axis_size("tm"), lax.axis_size("rate")
    piece = strain.shape[1]
    rows = piece // LANES
    bin_rows = psd_ref.shape[1] // LANES
    basis, taps = filters.shape[2:]
    templ = mixing.shape[2]
    nblk = nb * ntm
    slots = nr * nblk
    group = min(16, slots)
    quads = taps // LANES // 4
    share = templ // nr
    pad = -(-(taps // LANES + 1) // rows) * rows
    constants = dft_constants(piece, group)
    vmem = pl.BlockSpec(memory_space=pltpu.VMEM)
    smem = pl.BlockSpec(memory_space=pltpu.SMEM)
    out = jax.ShapeDtypeStruct((nb, share, piece), F32)
    return pl.pallas_call(
        functools.partial(kernel, (nb, ntm, nr, group)),
        out_shape=(out, out),
        in_specs=[vmem, vmem, smem, vmem, vmem, vmem, smem, vmem, vmem] + [vmem] * 5,
        out_specs=(vmem, vmem),
        scratch_shapes=[
            pltpu.VMEM((slots, 2 * rows, LANES), F32),
            pltpu.VMEM((nr, 2 * bin_rows, LANES), F32),
            pltpu.VMEM((nr, quads, 16, LANES), BF16),
            pltpu.VMEM((nr, quads, nb, 16, LANES), BF16),
            pltpu.VMEM((nr, pad + nblk * rows + rows, LANES), F32),
            pltpu.VMEM((slots, rows, LANES), F32),
            pltpu.VMEM((slots, rows, LANES), F32),
            pltpu.VMEM((slots, rows, LANES), F32),
            pltpu.VMEM((2 * nb, 3 * LANES), F32),
            pltpu.VMEM((2 * nb, LANES, 3 * LANES), BF16),
            pltpu.VMEM((2 * nb, LANES, 3 * LANES), BF16),
            pltpu.SemaphoreType.DMA((slots,)),
            pltpu.SemaphoreType.DMA((slots,)),
            pltpu.SemaphoreType.DMA((nr,)),
            pltpu.SemaphoreType.DMA((nr,)),
            pltpu.SemaphoreType.DMA((nb * nr,)),
            pltpu.SemaphoreType.DMA((nb * nr,)),
        ],
        compiler_params=pltpu.CompilerParams(
            collective_id=0, has_side_effects=True, vmem_limit_bytes=40 * 1024 * 1024
        ),
    )(
        strain.reshape(rows, LANES),
        gate_mask.reshape(rows, LANES),
        psd_reset,
        psd_ref.reshape(bin_rows, LANES),
        psd_rate.reshape(bin_rows, LANES),
        filters.reshape(basis, taps),
        basis_count,
        mixing.reshape(templ * 2, basis),
        autocorrelation,
        *constants,
    )


def solution(mesh):
    return jax.shard_map(
        body,
        mesh=mesh,
        in_specs=(
            P("rate", ("parts", "bank", "tm")),
            P(("parts", "bank", "tm")),
            P(("parts", "bank", "tm")),
            P("rate", None),
            P("rate", None),
            P("bank", "rate", None, None),
            P("bank"),
            P("bank", "rate", None, None, None),
            P(),
        ),
        out_specs=(
            P(None, "rate", ("parts", "bank", "tm")),
            P(None, "rate", ("parts", "bank", "tm")),
        ),
        check_vma=False,
    )
```

time: 249 us -> 27.3 us (0.11)
  local copies, waits for them, and re-layouts: 107 us -> 9.94 us
  blocking collectives: 69.6 us -> 0 us
  matrix products: 49.3 us -> 0 us
  Pallas kernels: 0 us -> 14.9 us
  starting transfers between devices: 11.3 us -> 0 us
  waiting for transfers between devices: 6.3 us -> 0 us
    all_gather x5 -> x0, blocking collectives: 69.6 us -> none  [the longest x2 53.8 us: entering(): gathered = jax.tree.map(lambda a: lax.all_gather(a, axis), part)]
    another operation x10 -> x0, local copies, waits for them, and re-layouts: 56.1 us -> none  [the longest x2 51.7 us: toeplitz_basis(): tiled = jnp.tile(spread, (1, frame_len))[:, :frame_len * line_len]]
    dot_general x8 -> x0, matrix products: 49.3 us -> none  [the longest x1 10.4 us: body(): jnp.dot(sin_table, imag_part * bin_scale, precision=HIGHEST)]
    unnamed x34 -> x26, local copies, waits for them, and re-layouts: 32 us -> 9.94 us
    slice x9 -> x0, local copies, waits for them, and re-layouts: 15.3 us -> none  [the longest x1 7.01 us: toeplitz_basis(): shifted[:, :, frame_len:frame_len + lag_count * frame_len]]
    pallas_call x0 -> x1, Pallas kernels: none -> 14.9 us  [body(): pl.pallas_call(functools.partial(kernel, (nb, ntm, nr, group)), out_shape...]
    ppermute x4 -> x0, starting transfers between devices: 7.98 us -> none  [the longest x1 4.55 us: extended_2(): lax.ppermute(lax.slice_in_dim(block, block.shape[dim] - width, None, axis...]
    all_to_all x1 -> x0, waiting for transfers between devices: 5.59 us -> none  [body(): lax.all_to_all(snr_part[None], 'bank', split_axis=3, concat_axis=0, tiled...]
  transfers between devices with their start and end apart: 5 -> 0, of which waited for: 2 -> 0; matrix products, arithmetic and copies ran while one was open for 39% -> 0% of each run, Pallas kernels for 0% -> 0%
where the time goes in v1:
time: 27.3 us; the launch traced here: 26.8 us
  Pallas kernels  14.9 us (55%)
  local copies, waits for them, and re-layouts  9.94 us (36%)
  between operations  1.98 us (7%)
    pallas_call x1, Pallas kernels, body(): pl.pallas_call(functools.partial(kernel, (nb, ntm, nr, group)), out_shape...  14.9 us
    unnamed x26, local copies, waits for them, and re-layouts  9.94 us

profile of v1, /device:TPU:0, one launch (start us, length us, event | category | flops | bytes accessed | tf_op | source)
XLA Modules:
  0.0 26.8 jit_solution(1266814153891782651)
XLA Ops:
  0.6 0.0 copy-start.5
  1.9 0.0 copy-start.9
  2.0 0.0 copy-done.5
  2.0 0.7 %copy-done.9 = f32[1,512]{1,0:T(1,128)S(1)} copy-done((f32[1,512]{1,0:T(1,128)S(1)}, f32[1,512]{1,0:T(1,128)}, u32[]{:S(2)}) %copy-start.9) | copy-done | bytes 2072
  2.6 0.0 copy-start
  2.6 0.9 %copy-done = f32[256,256]{1,0:T(8,128)S(1)} copy-done((f32[256,256]{1,0:T(8,128)S(1)}, f32[256,256]{1,0:T(8,128)}, u32[]{:S(2)}) %copy-start) | copy-done | bytes 262168
  3.6 0.0 copy-start.1
  3.6 0.9 %copy-done.1 = f32[256,256]{1,0:T(8,128)S(1)} copy-done((f32[256,256]{1,0:T(8,128)S(1)}, f32[256,256]{1,0:T(8,128)}, u32[]{:S(2)}) %copy-start.1) | copy-done | bytes 262168
  4.5 0.0 copy-start.2
  4.5 0.9 %copy-done.2 = bf16[1,1,32,2048]{3,2,1,0:T(8,128)(2,1)S(1)} copy-done((bf16[1,1,32,2048]{3,2,1,0:T(8,128)(2,1)S(1)}, bf16[1,1,32,2048]{3,2,1,0:T(8,128)(2,1)}, u32[]{:S(2)}) %copy-start.2) | copy-done | bytes 131096
  5.4 0.0 copy-start.3
  5.4 0.9 %copy-done.3 = f32[128,256]{1,0:T(8,128)S(1)} copy-done((f32[128,256]{1,0:T(8,128)S(1)}, f32[128,256]{1,0:T(8,128)}, u32[]{:S(2)}) %copy-start.3) | copy-done | bytes 131096
  6.3 0.0 copy-start.4
  6.3 0.9 %copy-done.4 = f32[256,128]{1,0:T(8,128)S(1)} copy-done((f32[256,128]{1,0:T(8,128)S(1)}, f32[256,128]{1,0:T(8,128)}, u32[]{:S(2)}) %copy-start.4) | copy-done | bytes 131096
  7.2 0.0 copy-start.6
  7.2 0.7 %copy-done.6 = f32[2,8,128]{2,1,0:T(8,128)S(1)} copy-done((f32[2,8,128]{2,1,0:T(8,128)S(1)}, f32[2,8,128]{2,1,0:T(8,128)}, u32[]{:S(2)}) %copy-start.6) | copy-done | bytes 8216
  7.9 0.0 copy-start.7
  7.9 0.7 %copy-done.7 = f32[1,1024]{1,0:T(1,128)S(1)} copy-done((f32[1,1024]{1,0:T(1,128)S(1)}, f32[1,1024]{1,0:T(1,128)}, u32[]{:S(2)}) %copy-start.7) | copy-done | bytes 4120
  8.6 0.0 copy-start.8
  8.6 0.7 %copy-done.8 = s32[1024]{0:T(1024)S(1)} copy-done((s32[1024]{0:T(1024)S(1)}, s32[1024]{0:T(1024)}, u32[]{:S(2)}) %copy-start.8) | copy-done | bytes 4120
  9.3 0.0 copy-start.10
  9.3 0.7 %copy-done.10 = f32[1,512]{1,0:T(1,128)S(1)} copy-done((f32[1,512]{1,0:T(1,128)S(1)}, f32[1,512]{1,0:T(1,128)}, u32[]{:S(2)}) %copy-start.10) | copy-done | bytes 2072
  10.0 0.0 copy-start.11
  10.0 0.7 %copy-done.11 = bf16[1,1,4,2,32]{4,3,2,1,0:T(2,128)(2,1)S(1)} copy-done((bf16[1,1,4,2,32]{4,3,2,1,0:T(2,128)(2,1)S(1)}, bf16[1,1,4,2,32]{4,3,2,1,0:T(2,128)(2,1)}, u32[]{:S(2)}) %copy-start.11) | copy-done | bytes 536
  10.7 14.9 %shard_map.149 = (f32[4,2,1024]{2,1,0:T(2,128)S(1)}, f32[4,2,1024]{2,1,0:T(2,128)S(1)}) custom-call(f32[8,128]{1,0:T(8,128)S(1)} %bitcast.7, s32[8,128]{1,0:T(8,128)S(1)} %bitcast.8, s32[1]{0:T(128)S(6)} %copy.18.reset, f32[4,128]{1,0:T(4,128)S(1)} %bitcast.9, f32[4,128]{1,0:T(4,128)S(1)} %bitcast.10, bf16[32,2048]{1,0:T(8,128)(2,1)S(1)} %bitcast.6, ...), custom_call_target="tpu_custom_call" | custom-call | tf_op jit(solution)/shard_map/pallas_call | solution.py:420
  25.6 0.6 %copy.20 = f32[4,2,1024]{2,1,0:T(2,128)} copy(f32[4,2,1024]{2,1,0:T(2,128)S(1)} %get-tuple-element.4) | data formatting | bytes 65536
  26.2 0.6 %copy.21 = f32[4,2,1024]{2,1,0:T(2,128)} copy(f32[4,2,1024]{2,1,0:T(2,128)S(1)} %get-tuple-element.5) | data formatting | bytes 65536
Async XLA Ops:
  0.6 1.3 %copy-start.5 = (f32[4,2,257]{2,1,0:T(2,128)S(1)}, f32[4,2,257]{2,1,0:T(2,128)}, u32[]{:S(2)}) copy-start(f32[4,2,257]{2,1,0:T(2,128)} %auto.1) | copy-start | bytes 24676
  1.9 0.7 %copy-start.9 = (f32[1,512]{1,0:T(1,128)S(1)}, f32[1,512]{1,0:T(1,128)}, u32[]{:S(2)}) copy-start(f32[1,512]{1,0:T(1,128)} %param.17) | copy-start | bytes 6148
  2.6 0.9 %copy-start = (f32[256,256]{1,0:T(8,128)S(1)}, f32[256,256]{1,0:T(8,128)}, u32[]{:S(2)}) copy-start(f32[256,256]{1,0:T(8,128)} %constant.13.clone.inverse) | copy-start | bytes 786436
  3.6 0.9 %copy-start.1 = (f32[256,256]{1,0:T(8,128)S(1)}, f32[256,256]{1,0:T(8,128)}, u32[]{:S(2)}) copy-start(f32[256,256]{1,0:T(8,128)} %constant.12.clone.forward) | copy-start | bytes 786436
  4.5 0.9 %copy-start.2 = (bf16[1,1,32,2048]{3,2,1,0:T(8,128)(2,1)S(1)}, bf16[1,1,32,2048]{3,2,1,0:T(8,128)(2,1)}, u32[]{:S(2)}) copy-start(bf16[1,1,32,2048]{3,2,1,0:T(8,128)(2,1)} %param.19) | copy-start | bytes 393220
  5.4 0.9 %copy-start.3 = (f32[128,256]{1,0:T(8,128)S(1)}, f32[128,256]{1,0:T(8,128)}, u32[]{:S(2)}) copy-start(f32[128,256]{1,0:T(8,128)} %constant.14.clone.last) | copy-start | bytes 393220
  6.3 0.9 %copy-start.4 = (f32[256,128]{1,0:T(8,128)S(1)}, f32[256,128]{1,0:T(8,128)}, u32[]{:S(2)}) copy-start(f32[256,128]{1,0:T(8,128)} %constant.10.clone.first) | copy-start | bytes 393220
  7.2 0.7 %copy-start.6 = (f32[2,8,128]{2,1,0:T(8,128)S(1)}, f32[2,8,128]{2,1,0:T(8,128)}, u32[]{:S(2)}) copy-start(f32[2,8,128]{2,1,0:T(8,128)} %constant.11.clone.twiddle) | copy-start | bytes 24580
  7.9 0.7 %copy-start.7 = (f32[1,1024]{1,0:T(1,128)S(1)}, f32[1,1024]{1,0:T(1,128)}, u32[]{:S(2)}) copy-start(f32[1,1024]{1,0:T(1,128)} %param.14) | copy-start | bytes 12292
  8.6 0.7 %copy-start.8 = (s32[1024]{0:T(1024)S(1)}, s32[1024]{0:T(1024)}, u32[]{:S(2)}) copy-start(s32[1024]{0:T(1024)} %param.15) | copy-start | bytes 12292
  9.3 0.7 %copy-start.10 = (f32[1,512]{1,0:T(1,128)S(1)}, f32[1,512]{1,0:T(1,128)}, u32[]{:S(2)}) copy-start(f32[1,512]{1,0:T(1,128)} %param.18) | copy-start | bytes 6148
  10.0 0.7 %copy-start.11 = (bf16[1,1,4,2,32]{4,3,2,1,0:T(2,128)(2,1)S(1)}, bf16[1,1,4,2,32]{4,3,2,1,0:T(2,128)(2,1)}, u32[]{:S(2)}) copy-start(bf16[1,1,4,2,32]{4,3,2,1,0:T(2,128)(2,1)} %param.21) | copy-start | bytes 1540

commit v2 on v1

--- a/solution.py
+++ b/solution.py
@@ -1,5 +1,4 @@
 import functools
-import math
 
 import jax
 import jax.numpy as jnp
@@ -61,42 +60,18 @@
     return lax.dot_general(a, b, (((1,), (1,)), ((), ())), preferred_element_type=F32)
 
 
-def kernel(
-    sizes,
-    strain,
-    gate,
-    reset,
-    ref,
-    rate,
-    filters,
-    count,
-    mixing,
-    auto,
-    first,
-    twiddle,
-    forward,
-    inverse,
-    last,
-    out_sq,
-    out_chi,
-    xbuf,
-    pbuf,
-    gsend,
-    gbuf,
-    wbuf,
-    lbuf,
-    yre,
-    yim,
-    rpad,
-    rhi,
-    rlo,
-    x_send,
-    x_recv,
-    p_send,
-    p_recv,
-    g_send,
-    g_recv,
-):
+def kernel(sizes, *refs):
+    sources, (out_sq, out_chi), held = refs[:14], refs[14:16], refs[16:30]
+    strain, gate, reset, ref, rate, filters, count, mixing, auto = held[:9]
+    first, twiddle, forward, inverse, last = held[9:]
+    (xbuf, pbuf, gsend, gbuf, wbuf, lbuf, yre, yim, rpad, rhi, rlo) = refs[30:41]
+    (x_send, x_recv, p_send, p_recv, g_send, g_recv, in_sem) = refs[41:]
+    loads = [
+        pltpu.make_async_copy(source, target, in_sem.at[i])
+        for i, (source, target) in enumerate(zip(sources, held))
+    ]
+    for load in loads:
+        load.start()
     nb, ntm, nr, group = sizes
     nblk = nb * ntm
     slots = nr * nblk
@@ -120,6 +95,8 @@
 
     each(slots - 1, greet)
 
+    for load in loads[:5]:
+        load.wait()
     xbuf[me, 0:rows, :] = strain[...] * gate[...].astype(F32)
     xbuf[me, rows : 2 * rows, :] = jnp.full((rows, LANES), reset[0], jnp.int32).astype(F32)
     bin_rows = ref.shape[0]
@@ -152,6 +129,8 @@
     for i in range(nr - 1):
         p_copy(core, lax.rem(core + i + 1, nr), i).start()
 
+    for load in loads[5:]:
+        load.wait()
     basis = filters.shape[0]
     mix_rows = mixing.shape[0]
     share = mix_rows // nr // 2
@@ -239,7 +218,7 @@
         jnp.where((lane == 0) & (iota((rows, LANES), 0) == 0), 1.0 / length, 2.0 / length),
         0.0,
     )
-    refs = [jnp.where(live_bin, psd[2 * c * rows : (2 * c + 1) * rows], 1.0) for c in range(nr)]
+    levels = [jnp.where(live_bin, psd[2 * c * rows : (2 * c + 1) * rows], 1.0) for c in range(nr)]
     rates = [psd[(2 * c + 1) * rows : (2 * c + 2) * rows] for c in range(nr)]
 
     tall = group * rows
@@ -262,13 +241,13 @@
         for c in range(nr):
             at = c * nblk + i
             keep = (1.0 - rates[c]) * (1.0 - 0.5 * xbuf[at, rows : 2 * rows, :])
-            level = jnp.log(lbuf[at] + 0.1 * refs[c])
+            level = jnp.log(lbuf[at] + 0.1 * levels[c])
             state = keep * states[c] + rates[c] * level
             lbuf[at] = jnp.exp(-0.5 * state) * weight
             after.append(state)
         return tuple(after)
 
-    states = tuple(jnp.log(refs[c]) for c in range(nr))
+    states = tuple(jnp.log(levels[c]) for c in range(nr))
     if nblk <= 16:
         for i in range(nblk):
             states = advance(i, states)
@@ -415,14 +394,27 @@
     pad = -(-(taps // LANES + 1) // rows) * rows
     constants = dft_constants(piece, group)
     vmem = pl.BlockSpec(memory_space=pltpu.VMEM)
-    smem = pl.BlockSpec(memory_space=pltpu.SMEM)
     out = jax.ShapeDtypeStruct((nb, share, piece), F32)
+    operands = (
+        strain.reshape(rows, LANES),
+        gate_mask.reshape(rows, LANES),
+        psd_reset,
+        psd_ref.reshape(bin_rows, LANES),
+        psd_rate.reshape(bin_rows, LANES),
+        filters.reshape(basis, taps),
+        basis_count,
+        mixing.reshape(templ * 2, basis),
+        autocorrelation,
+        *constants,
+    )
+    held = [(pltpu.SMEM if a.ndim == 1 else pltpu.VMEM)(a.shape, a.dtype) for a in operands]
     return pl.pallas_call(
         functools.partial(kernel, (nb, ntm, nr, group)),
         out_shape=(out, out),
-        in_specs=[vmem, vmem, smem, vmem, vmem, vmem, smem, vmem, vmem] + [vmem] * 5,
+        in_specs=[pl.BlockSpec(memory_space=pltpu.HBM)] * len(operands),
         out_specs=(vmem, vmem),
-        scratch_shapes=[
+        scratch_shapes=held
+        + [
             pltpu.VMEM((slots, 2 * rows, LANES), F32),
             pltpu.VMEM((nr, 2 * bin_rows, LANES), F32),
             pltpu.VMEM((nr, quads, 16, LANES), BF16),
@@ -440,22 +432,12 @@
             pltpu.SemaphoreType.DMA((nr,)),
             pltpu.SemaphoreType.DMA((nb * nr,)),
             pltpu.SemaphoreType.DMA((nb * nr,)),
+            pltpu.SemaphoreType.DMA((len(operands),)),
         ],
         compiler_params=pltpu.CompilerParams(
-            collective_id=0, has_side_effects=True, vmem_limit_bytes=40 * 1024 * 1024
+            collective_id=0, has_side_effects=True, vmem_limit_bytes=62 * 1024 * 1024
         ),
-    )(
-        strain.reshape(rows, LANES),
-        gate_mask.reshape(rows, LANES),
-        psd_reset,
-        psd_ref.reshape(bin_rows, LANES),
-        psd_rate.reshape(bin_rows, LANES),
-        filters.reshape(basis, taps),
-        basis_count,
-        mixing.reshape(templ * 2, basis),
-        autocorrelation,
-        *constants,
-    )
+    )(*operands)
 
 
 def solution(mesh):

time: 27.3 us -> 19.9 us (0.73); the launches traced: 26.8 us -> 19.7 us
  local copies, waits for them, and re-layouts: 9.94 us -> 2 us
  Pallas kernels: 14.9 us -> 15.8 us
    unnamed x26 -> x4, local copies, waits for them, and re-layouts: 9.94 us -> 2 us
    pallas_call x1, Pallas kernels: 14.9 us -> 15.8 us  [body(): pl.pallas_call(functools.partial(kernel, (nb, ntm, nr, group)), out_shape...]
where the time goes in v2:
time: 19.9 us; the launch traced here: 19.7 us
  Pallas kernels  15.8 us (79%)
  local copies, waits for them, and re-layouts  2 us (10%)
  between operations  1.94 us (10%)
    pallas_call x1, Pallas kernels, body(): pl.pallas_call(functools.partial(kernel, (nb, ntm, nr, group)), out_shape...  15.8 us
    unnamed x4, local copies, waits for them, and re-layouts  2 us

profile of v2, /device:TPU:0, one launch (start us, length us, event | category | flops | bytes accessed | tf_op | source)
XLA Modules:
  0.0 19.7 jit_solution(5760922482236629660)
XLA Ops:
  1.9 15.8 %shard_map.149 = (f32[4,2,1024]{2,1,0:T(2,128)}, f32[4,2,1024]{2,1,0:T(2,128)}) custom-call(f32[8,128]{1,0:T(8,128)} %bitcast.7, s32[8,128]{1,0:T(8,128)} %bitcast.8, s32[1]{0:T(128)S(6)} %copy.18.refs_2_, f32[4,128]{1,0:T(4,128)} %bitcast.9, f32[4,128]{1,0:T(4,128)} %bitcast.10, bf16[32,2048]{1,0:T(8,128)(2,1)} %bitcast.6, s32[1]{0:T(128)S(6)} %copy.19.refs_6_, ...), custom_call_target="tpu_custom_call" | custom-call | tf_op jit(solution)/shard_map/pallas_call | solution.py:411
  17.7 0.0 copy-start
  17.7 1.4 %copy.20 = f32[4,2,1024]{2,1,0:T(2,128)} copy(f32[4,2,1024]{2,1,0:T(2,128)} %get-tuple-element.4) | data formatting | bytes 65536
  19.1 0.0 copy-done
  19.1 0.6 %copy.21 = f32[4,2,1024]{2,1,0:T(2,128)} copy(f32[4,2,1024]{2,1,0:T(2,128)S(1)} %copy-done) | data formatting | bytes 65536
Async XLA Ops:
  17.7 1.4 %copy-start = (f32[4,2,1024]{2,1,0:T(2,128)S(1)}, f32[4,2,1024]{2,1,0:T(2,128)}, u32[]{:S(2)}) copy-start(f32[4,2,1024]{2,1,0:T(2,128)} %get-tuple-element.5) | copy-start | bytes 98308

commit v3 on v2

--- a/solution.py
+++ b/solution.py
@@ -61,11 +61,11 @@
 
 
 def kernel(sizes, *refs):
-    sources, (out_sq, out_chi), held = refs[:14], refs[14:16], refs[16:30]
+    sources, out, held = refs[:14], refs[14], refs[15:29]
     strain, gate, reset, ref, rate, filters, count, mixing, auto = held[:9]
     first, twiddle, forward, inverse, last = held[9:]
-    (xbuf, pbuf, gsend, gbuf, wbuf, lbuf, yre, yim, rpad, rhi, rlo) = refs[30:41]
-    (x_send, x_recv, p_send, p_recv, g_send, g_recv, in_sem) = refs[41:]
+    (xbuf, pbuf, gsend, gbuf, wbuf, lbuf, yre, yim, rpad, rhi, rlo) = refs[29:40]
+    (x_send, x_recv, p_send, p_recv, g_send, g_recv, in_sem) = refs[40:]
     loads = [
         pltpu.make_async_copy(source, target, in_sem.at[i])
         for i, (source, target) in enumerate(zip(sources, held))
@@ -362,14 +362,14 @@
         own = centre * centre
         lag = jnp.where(even, lag_energy[2 * j], lag_energy[2 * j + 1])
         value = summed - 2.0 * centre * corr + own * lag
-        chi = (value + pltpu.roll(value, height - 2, 0)) / (2 * window + 1)
+        chi = value + pltpu.roll(value, height - 2, 0)
         energy = own + pltpu.roll(own, height - 2, 0)
         for f in range(rows):
             for half in range(2):
                 at = 8 * f + 4 * half
                 cols = slice(f * LANES, (f + 1) * LANES)
-                out_sq[2 * j + half, :, cols] = energy[at : at + share]
-                out_chi[2 * j + half, :, cols] = chi[at : at + share]
+                out[0, 2 * j + half, :, cols] = energy[at : at + share]
+                out[1, 2 * j + half, :, cols] = chi[at : at + share]
 
     for i in range(nr - 1):
         p_copy(core, lax.rem(core + i + 1, nr), i).wait_send()
@@ -394,7 +394,7 @@
     pad = -(-(taps // LANES + 1) // rows) * rows
     constants = dft_constants(piece, group)
     vmem = pl.BlockSpec(memory_space=pltpu.VMEM)
-    out = jax.ShapeDtypeStruct((nb, share, piece), F32)
+    out = jax.ShapeDtypeStruct((2, nb, share, piece), F32)
     operands = (
         strain.reshape(rows, LANES),
         gate_mask.reshape(rows, LANES),
@@ -408,11 +408,11 @@
         *constants,
     )
     held = [(pltpu.SMEM if a.ndim == 1 else pltpu.VMEM)(a.shape, a.dtype) for a in operands]
-    return pl.pallas_call(
+    both = pl.pallas_call(
         functools.partial(kernel, (nb, ntm, nr, group)),
-        out_shape=(out, out),
+        out_shape=out,
         in_specs=[pl.BlockSpec(memory_space=pltpu.HBM)] * len(operands),
-        out_specs=(vmem, vmem),
+        out_specs=vmem,
         scratch_shapes=held
         + [
             pltpu.VMEM((slots, 2 * rows, LANES), F32),
@@ -438,6 +438,7 @@
             collective_id=0, has_side_effects=True, vmem_limit_bytes=62 * 1024 * 1024
         ),
     )(*operands)
+    return both[0], both[1] / autocorrelation.shape[2]
 
 
 def solution(mesh):

time: 19.9 us -> 19.3 us (0.970)
  local copies, waits for them, and re-layouts: 2 us -> 0 us
  other arithmetic: 0 us -> 1.42 us
    unnamed x4 -> x0, local copies, waits for them, and re-layouts: 2 us -> none
    div x0 -> x1, other arithmetic: none -> 1.42 us  [body(): return (both[0], both[1] / autocorrelation.shape[2])]
where the time goes in v3:
time: 19.3 us; the launch traced here: 19.1 us
  Pallas kernels  15.8 us (82%)
  between operations  1.93 us (10%)
  other arithmetic  1.42 us (7%)
    pallas_call x1, Pallas kernels, body(): pl.pallas_call(functools.partial(kernel, (nb, ntm, nr, group)), out_shape...  15.8 us
    div x1, other arithmetic, body(): return (both[0], both[1] / autocorrelation.shape[2])  1.42 us

profile of v3, /device:TPU:0, one launch (start us, length us, event | category | flops | bytes accessed | tf_op | source)
XLA Modules:
  0.0 19.1 jit_solution(7430748759404947999)
XLA Ops:
  1.9 15.8 %shard_map.149 = f32[2,4,2,1024]{3,2,1,0:T(2,128)} custom-call(f32[8,128]{1,0:T(8,128)} %bitcast.11, s32[8,128]{1,0:T(8,128)} %bitcast.12, s32[1]{0:T(128)S(6)} %copy.16.refs_2_, f32[4,128]{1,0:T(4,128)} %bitcast.13, f32[4,128]{1,0:T(4,128)} %bitcast.14, bf16[32,2048]{1,0:T(8,128)(2,1)} %bitcast.10, s32[1]{0:T(128)S(6)} %copy.17.refs_6_, ...), custom_call_target="tpu_custom_call" | custom-call | tf_op jit(solution)/shard_map/pallas_call | solution.py:411
  17.7 1.4 %multiply_bitcast_fusion = (f32[4,2,1024]{2,1,0:T(2,128)}, f32[4,2,1024]{2,1,0:T(2,128)}) fusion(f32[2,4,2,1024]{3,2,1,0:T(2,128)} %shard_map.149), kind=kLoop, calls=%fused_computation | loop fusion | flops 8192 | bytes 131072 | tf_op jit(solution)/shard_map/div | solution.py:441
